TPU v7x, 256 devices: a whole 4x4x8 slice. The times are simulated.
256 devices in a mesh: layer: 16 (over z, core), row: 4 (over x), col: 4 (over y).
Axes of the slice: x: 4, y: 4, z: 8, core: 2. Of those that a mesh axis runs over, the one named last changes fastest.
Arguments:
- lower_panels: bfloat16 [48, 5120, 2048], P('layer', 'row', 'col'), may hold values from -4 to 4
- upper_panels: bfloat16 [48, 5120, 2048], P('layer', 'col', 'row'), may hold values from -0.125 to 0.125
- lower_lists: int32 [16, 2], P('layer'), may hold values from 0 to 2
- upper_lists: int32 [16, 2], P('layer'), may hold values from 0 to 2
- block_counts: int32 [16], P('layer'), may hold values from 1 to 2, as said below
- ancestor: bfloat16 [320, 16, 5120], P('row', 'layer', 'col'), may hold values from -6 to 6
- pivot_inverse: float32 [320, 16], P('row', 'layer'), may hold values from 0.3 to 3
Outputs:
- updated: float32 [320, 16, 5120], P('row', 'layer', 'col')
Inputs may be any that keep to these rules, and one draw needn't show every extreme that they name: `block_counts`: each layer lists at least one pair; some layer lists exactly 2 and some layer exactly one. `lower_lists`: entries at slots from a layer's count onward are ignored. `upper_lists`: entries at slots from a layer's count onward are ignored.
All inputs are finite; a program needn't handle non-finite values.
Results may differ from a plain program's by a relative error of at most 0.0003.
Values may be sent and summed in bfloat16 or wider, within the bound.
A program may use at most 128 MiB of HBM per device.

v0:
```python
import jax
import jax.numpy as jnp
from jax import lax
from jax.sharding import PartitionSpec as P


def per_device(
    lower_panels, upper_panels, lower_lists, upper_lists, block_counts, ancestor, pivot_inverse
):
    listed = lower_lists.shape[1]
    pairs_here = block_counts[0]
    rows_here = lower_panels.shape[1]
    cols_here = upper_panels.shape[1]
    layer_count = lax.axis_size("layer")
    groups_here = rows_here // layer_count
    slots = jnp.arange(listed, dtype=jnp.int32)
    live = slots < pairs_here
    lower_chosen = jnp.take(lower_panels, lower_lists[0], axis=0)
    lower_chosen = jnp.where(live[:, None, None], lower_chosen, jnp.zeros((), lower_chosen.dtype))
    upper_chosen = jnp.take(upper_panels, upper_lists[0], axis=0)
    upper_full = lax.all_gather(upper_chosen, "row", axis=2, tiled=True)
    lower_full = lax.all_gather(lower_chosen, "col", axis=2, tiled=True)
    inner_width = lower_full.shape[2]
    reordered = lower_full.reshape(listed, groups_here, layer_count, inner_width)
    reordered = jnp.transpose(reordered, (0, 2, 1, 3)).reshape(listed, rows_here, inner_width)
    mine = lax.psum_scatter(
        lax.dot_general(
            reordered, upper_full, (((0, 2), (0, 2)), ((), ())), preferred_element_type=jnp.float32
        ),
        "layer",
        scatter_dimension=0,
        tiled=True,
    )
    summed = mine.reshape(groups_here, 1, cols_here)
    return (ancestor.astype(jnp.float32) - summed) * pivot_inverse[:, :, None]


def solution(mesh):
    in_specs = (
        P("layer", "row", "col"),
        P("layer", "col", "row"),
        P("layer", None),
        P("layer", None),
        P("layer"),
        P("row", "layer", "col"),
        P("row", "layer"),
    )
    out_specs = P("row", "layer", "col")
    return jax.shard_map(
        per_device, mesh=mesh, in_specs=in_specs, out_specs=out_specs, check_vma=False
    )
```

profile of v0, /device:TPU:8, one launch (start us, length us, event | category | flops | bytes accessed | tf_op | source)
XLA Modules:
  0.0 323.6 jit_solution(16516560918264088968)
XLA Ops:
  6.5 0.0 all-gather.3.cloned.1.call-start
  7.2 0.7 compare_select_fusion.1
  7.8 0.7 compare_and_fusion.1
  8.5 2.8 gather_fusion
  11.4 1.9 select_select_fusion
  13.2 0.0 copy-start.2
  13.2 0.0 all-gather.3.cloned.1.call-update
  13.3 0.0 all-gather.5.cloned.1.call-start
  13.3 0.6 copy-done.2
  13.9 2.8 gather_fusion.1
  16.8 1.8 broadcast_select_fusion
  18.6 0.0 all-gather.5.cloned.1.call-update
  18.6 0.0 reduce-scatter.2.cloned.1.call-start
  18.6 101.1 %all-gather.3.cloned.1.call-done = bf16[2,1280,2048]{2,1,0:T(8,128)(2,1)} async-done(((bf16[2,1280,512]{2,1,0:T(8,128)(2,1)}), bf16[2,1280,2048]{2,1,0:T(8,128)(2,1)}) %all-gather.3.cloned.1.call-update) | async-done | bytes 10485776 | tf_op jit(solution)/shard_map/all_gather | solution.py:22
  119.7 13.7 %copy.8 = bf16[2,80,16,2048]{3,1,2,0:T(8,128)(2,1)} copy(bf16[2,80,16,2048]{3,2,1,0:T(8,128)(2,1)} %bitcast.23) | data formatting | bytes 20971520 | tf_op jit(solution)/shard_map/reshape | solution.py:24
  133.5 92.5 %all-gather.5.cloned.1.call-done = bf16[2,1280,2048]{2,1,0:T(8,128)(2,1)} async-done(((bf16[2,1280,512]{2,1,0:T(8,128)(2,1)}), bf16[2,1280,2048]{2,1,0:T(8,128)(2,1)}) %all-gather.5.cloned.1.call-update) | async-done | bytes 10485776 | tf_op jit(solution)/shard_map/all_gather | solution.py:21
  226.0 20.3 %convolution_bitcast_fusion = f32[1280,1280]{1,0:T(8,128)} fusion(bf16[2,1280,2048]{2,1,0:T(8,128)(2,1)} %bitcast.24, bf16[2,1280,2048]{2,1,0:T(8,128)(2,1)} %all-gather.5.cloned.1.call-done), kind=kOutput, calls=%fused_computation.2 | convolution fusion | flops 13421772800 | bytes 27525120 | tf_op jit(solution)/shard_map/dot_general | solution.py:27
  246.3 0.0 copy-start
  246.3 0.0 copy-start.1
  246.3 0.0 reduce-scatter.2.cloned.1.call-update
  246.3 68.5 %reduce-scatter.2.cloned.1.call-done = f32[80,1280]{1,0:T(8,128)} async-done(((f32[1280,1280]{1,0:T(8,128)}), f32[80,1280]{1,0:T(8,128)}) %reduce-scatter.2.cloned.1.call-update) | async-done | bytes 409616 | tf_op jit(solution)/shard_map/reduce_scatter | solution.py:26
  314.8 0.0 copy-done
  314.8 0.0 copy-done.1
  314.8 1.1 fusion
  315.9 1.2 copy.9
  (4 shorter events, 0.0 us)
Async XLA Ops:
  6.5 113.2 %all-gather.3.cloned.1.call-start = ((), (), s32[]{:S(2)}) async-start(), calls=%async_computation.1 | async-start | bytes 13107200 | tf_op jit(solution)/shard_map/all_gather | solution.py:22
  13.2 0.7 copy-start.2
  13.3 212.7 %all-gather.5.cloned.1.call-start = ((), (), s32[]{:S(2)}) async-start(), calls=%async_computation.2 | async-start | bytes 13107200 | tf_op jit(solution)/shard_map/all_gather | solution.py:21
  18.6 296.2 %reduce-scatter.2.cloned.1.call-start = ((), (), s32[]{:S(2)}) async-start(), calls=%async_computation.3 | async-start | bytes 6963200 | tf_op jit(solution)/shard_map/reduce_scatter | solution.py:26
  246.3 68.5 %copy-start = (bf16[80,1,1280]{2,0,1:T(8,128)(2,1)S(1)}, bf16[80,1,1280]{2,0,1:T(8,128)(2,1)}, u32[]{:S(2)}) copy-start(bf16[80,1,1280]{2,0,1:T(8,128)(2,1)} %param.14) | copy-start | bytes 614404
  246.3 68.5 %copy-start.1 = (f32[80,1]{0,1:T(1,128)S(1)}, f32[80,1]{0,1:T(1,128)}, u32[]{:S(2)}) copy-start(f32[80,1]{0,1:T(1,128)} %param.15) | copy-start | bytes 964
Sparse Core Ops, SparseCore 0:
  13.4 106.2 all-gather.2
  121.5 104.3 all-gather.4
  246.5 68.2 reduce-scatter.1
where the time goes:
time: 324 us
  waiting for transfers between devices  262 us (81%)
  local copies, waits for them, and re-layouts  21.2 us (7%)
  matrix products  20.3 us (6%)
  between operations  13.8 us (4%)
  other arithmetic  6.14 us (2%)
    all_gather x1, waiting for transfers between devices, per_device(): lower_full = lax.all_gather(lower_chosen, 'col', axis=2, tiled=True)  101 us
    all_gather x1, waiting for transfers between devices, per_device(): upper_full = lax.all_gather(upper_chosen, 'row', axis=2, tiled=True)  92.5 us
    reduce_scatter x1, waiting for transfers between devices, per_device(): lax.psum_scatter(lax.dot_general(reordered, upper_full, (((0, 2), (0, 2))...  68.5 us
    dot_general x1, matrix products, per_device(): lax.dot_general(reordered, upper_full, (((0, 2), (0, 2)), ((), ())), pref...  20.3 us
    reshape x1, local copies, waits for them, and re-layouts, per_device(): lower_full.reshape(listed, groups_here, layer_count, inner_width)  13.7 us
  transfers between devices with their start and end apart: 3, of which 3 were waited for; matrix products, arithmetic and copies ran while one was open for 6% of the time, Pallas kernels for 0%

commit v1 on v0

v1 whole, which is shorter than its diff:
```python
import jax
import jax.numpy as jnp
from jax import lax
from jax.experimental import pallas as pl
from jax.experimental.pallas import tpu as pltpu
from jax.sharding import PartitionSpec as P

MESH = pl.DeviceIdType.MESH
GROUP = 128
CHUNKS = (128, 128, 256, 256, 256, 128, 128)
DIRECT = (0, 0, 0, 0, 0, 1, 1)
AHEAD = 2
NT = (((1,), (1,)), ((), ()))


def kernel(
    lower_list, upper_list, count, lower_hbm, upper_hbm, ancestor, pivots, out,
    first_lower, first_upper, rest_lower, rest_upper, lower_all, upper_all, product, from_core, from_z,
    load_sem, own_send, own_recv, fwd_send, fwd_recv, core_send, core_recv, z_send, z_recv,
):
    layer, x, y = lax.axis_index("layer"), lax.axis_index("row"), lax.axis_index("col")
    z, core = lax.div(layer, 2), lax.rem(layer, 2)
    sign = 1 - 2 * core
    starts = [sum(CHUNKS[:i]) for i in range(len(CHUNKS))]
    last = len(CHUNKS) - 1
    first = CHUNKS[0]
    total_rows = lower_hbm.shape[1]

    loads = []
    for i, (hbm, head, rest) in enumerate(
        ((lower_hbm, first_lower, rest_lower), (upper_hbm, first_upper, rest_upper))
    ):
        loads.append(pltpu.make_async_copy(hbm.at[:, pl.ds(0, first)], head, load_sem.at[i, 0]))
        loads.append(
            pltpu.make_async_copy(hbm.at[:, pl.ds(first, total_rows - first)], rest, load_sem.at[i, 1])
        )
    for i in (0, 2, 1, 3):
        loads[i].start()

    def at_z(distance):
        return {"layer": lax.rem(layer + 2 * distance + 32, 16)}

    def at_ring(axis, step):
        return {"col": lax.rem(y + step + 4, 4)} if axis == 0 else {"row": lax.rem(x + step + 4, 4)}

    barrier = pltpu.get_barrier_semaphore()
    met = [at_ring(a, s) for a in (0, 1) for s in (1, -1)] + [{"layer": layer + sign}]
    met += [at_z(d) for d in range(1, 8)]
    for target in met:
        pl.semaphore_signal(barrier, inc=1, device_id=target, device_id_type=MESH)

    position = lax.broadcasted_iota(jnp.int32, (GROUP, GROUP), 0)
    source = lax.broadcasted_iota(jnp.int32, (GROUP, GROUP), 1)
    wanted = (position % 8) * 16 + ((position // 8) % 8) * 2 + position // 64
    place = jnp.where(wanted == source, 1.0, 0.0).astype(jnp.bfloat16)
    buffers = (lower_all, upper_all)
    mine = (y, x)

    def prepare(i):
        low, up = (first_lower, first_upper) if i == 0 else (rest_lower, rest_upper)
        offset = 0 if i == 0 else first
        for slot in range(2):
            live = slot < count[0]
            lo, uo = lower_list[0, slot], upper_list[0, slot]
            for g in range(CHUNKS[i] // GROUP):
                row = starts[i] + g * GROUP
                rows = pl.ds(row - offset, GROUP)
                moved = jnp.dot(place, low[lo, rows, :], preferred_element_type=jnp.float32)
                moved = jnp.where(live, moved, 0.0)
                lower_all[y, slot, pl.ds(row, GROUP), :] = moved.astype(jnp.bfloat16)
                upper_all[x, slot, pl.ds(row, GROUP), :] = up[uo, rows, :]

    def own(axis, way, i, origin):
        step = 1 - 2 * way
        part = buffers[axis].at[origin, :, pl.ds(starts[i], CHUNKS[i]), :]
        return pltpu.make_async_remote_copy(
            part, part, own_send.at[axis, way, i], own_recv.at[axis, way, i],
            device_id=at_ring(axis, step), device_id_type=MESH,
        )

    def fwd(axis, way, i, origin):
        step = 1 - 2 * way
        part = buffers[axis].at[origin, way, pl.ds(starts[i], CHUNKS[i]), :]
        return pltpu.make_async_remote_copy(
            part, part, fwd_send.at[axis, way, i], fwd_recv.at[axis, way, i],
            device_id=at_ring(axis, step), device_id_type=MESH,
        )

    links = [(axis, way) for way in (0, 1) for axis in (0, 1)]

    def send_own(i):
        for axis, way in links:
            own(axis, way, i, mine[axis]).start()

    def pass_on(i):
        for axis, way in links:
            origin = lax.rem(mine[axis] - (1 - 2 * way) + 4, 4)
            own(axis, way, i, origin).wait_recv()
            fwd(axis, way, i, origin).start()

    def wait_far(i):
        for axis, way in links:
            fwd(axis, way, i, lax.rem(mine[axis] + 2, 4)).wait_recv()

    def block(row, rows, col, cols):
        total = None
        for j in range(4):
            for slot in range(2):
                term = lax.dot_general(
                    lower_all[j, slot, pl.ds(row, rows), :], upper_all[j, slot, pl.ds(col, cols), :],
                    NT, preferred_element_type=jnp.float32,
                )
                total = term if total is None else total + term
        for g in range(rows // GROUP):
            where = row // 16 + g * 8
            if not isinstance(where, int):
                where = pl.multiple_of(where, 8)
            product[:, :, pl.ds(where, 8), pl.ds(col, cols)] = total[g * GROUP : (g + 1) * GROUP].reshape(
                2, 8, 8, cols
            )

    def down(i):
        end, col, cols = starts[i] + CHUNKS[i], starts[i], CHUNKS[i]
        if end >= 256:

            @pl.loop(0, end // 256)
            def _(t):
                block(pl.multiple_of(t * 256, 256), 256, col, cols)

        if end % 256:
            block(end // 256 * 256, end % 256, col, cols)

    def across(i):
        row, rows, end = starts[i], CHUNKS[i], starts[i]
        if end >= 256:

            @pl.loop(0, end // 256)
            def _(t):
                block(row, rows, pl.multiple_of(t * 256, 256), 256)

        if end % 256:
            block(row, rows, end // 256 * 256, end % 256)

    def rect(i, k):
        begin, end = starts[i], starts[i] + CHUNKS[i]
        if k == 0:
            return pl.ds(0, end // 16), pl.ds(begin, end - begin)
        return pl.ds(begin // 16, (end - begin) // 16), pl.ds(0, begin)

    def to_core(i, k):
        rows, cols = rect(i, k)
        return pltpu.make_async_remote_copy(
            product.at[1 - core, :, rows, cols], from_core.at[:, rows, cols],
            core_send.at[i, k], core_recv.at[i, k],
            device_id={"layer": layer + sign}, device_id_type=MESH,
        )

    def to_z(i, k, slot, target, hop):
        rows, cols = rect(i, k)
        return pltpu.make_async_remote_copy(
            product.at[core, lax.rem(z + target + 16, 8), rows, cols], from_z.at[slot, rows, cols],
            z_send.at[i, k, slot], z_recv.at[i, k, slot],
            device_id=at_z(hop), device_id_type=MESH,
        )

    def parts(i):
        return (0, 1) if i else (0,)

    def add_core(i, k):
        to_core(i, k).wait_recv()
        rows, cols = rect(i, k)

        @pl.loop(0, 8)
        def _(t):
            product[core, t, rows, cols] = product[core, t, rows, cols] + from_core[t, rows, cols]

    def add_z(i, k, slot, target):
        rows, cols = rect(i, k)
        at = lax.rem(z + target + 16, 8)
        product[core, at, rows, cols] = product[core, at, rows, cols] + from_z[slot, rows, cols]

    def advance(i, step):
        for k in parts(i):
            if step == 0:
                add_core(i, k)
            if DIRECT[i]:
                for d in (4, 3, 5, 2, 6, 1, 7):
                    if step == 0:
                        to_z(i, k, d - 1, d, d).start()
                    else:
                        to_z(i, k, d - 1, d, d).wait_recv()
                        add_z(i, k, d - 1, 0)
                continue
            if step:
                to_z(i, k, step - 1, 0, sign).wait_recv()
                add_z(i, k, step - 1, sign * (4 - step))
            if step < 4:
                to_z(i, k, step, sign * (4 - step), sign).start()
            if 0 < step < 4:
                to_z(i, k, 3 + step, 0, -sign).wait_recv()
                add_z(i, k, 3 + step, -sign * (3 - step))
            if step < 3:
                to_z(i, k, 4 + step, -sign * (3 - step), -sign).start()

    def steps(i):
        return 2 if DIRECT[i] else 5

    pending = []

    def advance_all(count):
        for _ in range(count):
            for entry in list(pending):
                advance(entry[0], entry[1])
                entry[1] += 1
                if entry[1] == steps(entry[0]):
                    pending.remove(entry)

    def finish(i):
        wait_far(i)
        down(i)
        to_core(i, 0).start()
        if i:
            across(i)
            to_core(i, 1).start()

    loads[0].wait()
    loads[2].wait()
    prepare(0)
    pl.semaphore_wait(barrier, len(met))
    send_own(0)
    loads[1].wait()
    loads[3].wait()
    for i in range(1, AHEAD):
        prepare(i)
        send_own(i)
    for i in range(last + 1):
        if i + AHEAD <= last:
            prepare(i + AHEAD)
            send_own(i + AHEAD)
        pass_on(i)
        if i:
            finish(i - 1)
            advance_all(1)
            pending.append([i - 1, 0])
    finish(last)
    pending.append([last, 0])
    advance_all(5)

    @pl.loop(0, total_rows // 256)
    def _(t):
        rows = pl.ds(pl.multiple_of(t * 16, 16), 16)
        rest = ancestor[rows, :].astype(jnp.float32) - product[core, z, rows, :]
        out[rows, :] = rest * pivots[rows, :]

    for i in range(last + 1):
        for axis, way in links:
            own(axis, way, i, mine[axis]).wait_send()
            fwd(axis, way, i, lax.rem(mine[axis] - (1 - 2 * way) + 4, 4)).wait_send()
        for k in parts(i):
            to_core(i, k).wait_send()
            for slot in range(7):
                if DIRECT[i]:
                    to_z(i, k, slot, slot + 1, slot + 1).wait_send()
                elif slot < 4:
                    to_z(i, k, slot, sign * (4 - slot), sign).wait_send()
                else:
                    to_z(i, k, slot, -sign * (7 - slot), -sign).wait_send()


def per_device(
    lower_panels, upper_panels, lower_lists, upper_lists, block_counts, ancestor, pivot_inverse
):
    pool, rows, width = lower_panels.shape
    groups, _, cols = ancestor.shape
    chunks = len(CHUNKS)
    smem = pl.BlockSpec(memory_space=pltpu.SMEM)
    vmem = pl.BlockSpec(memory_space=pltpu.VMEM)
    hbm = pl.BlockSpec(memory_space=pl.ANY)
    dma = pltpu.SemaphoreType.DMA
    updated = pl.pallas_call(
        kernel,
        out_shape=jax.ShapeDtypeStruct((groups, cols), jnp.float32),
        in_specs=[smem, smem, smem, hbm, hbm, vmem, vmem],
        out_specs=vmem,
        scratch_shapes=[
            pltpu.VMEM((pool, CHUNKS[0], width), jnp.bfloat16),
            pltpu.VMEM((pool, CHUNKS[0], width), jnp.bfloat16),
            pltpu.VMEM((pool, rows - CHUNKS[0], width), jnp.bfloat16),
            pltpu.VMEM((pool, rows - CHUNKS[0], width), jnp.bfloat16),
            pltpu.VMEM((4, 2, rows, width), jnp.bfloat16),
            pltpu.VMEM((4, 2, cols, width), jnp.bfloat16),
            pltpu.VMEM((2, 8, groups, cols), jnp.float32),
            pltpu.VMEM((8, groups, cols), jnp.float32),
            pltpu.VMEM((7, groups, cols), jnp.float32),
            dma((2, 2)),
            dma((2, 2, chunks)),
            dma((2, 2, chunks)),
            dma((2, 2, chunks)),
            dma((2, 2, chunks)),
            dma((chunks, 2)),
            dma((chunks, 2)),
            dma((chunks, 2, 7)),
            dma((chunks, 2, 7)),
        ],
        compiler_params=pltpu.CompilerParams(
            collective_id=0, has_side_effects=True, vmem_limit_bytes=58 * 2**20
        ),
        cost_estimate=pl.CostEstimate(
            flops=4 * rows * cols * width * 4, bytes_accessed=9 * 2**20, transcendentals=0
        ),
    )(
        lower_lists, upper_lists, block_counts, lower_panels, upper_panels,
        ancestor.reshape(groups, cols), pivot_inverse,
    )
    return updated.reshape(groups, 1, cols)


def solution(mesh):
    in_specs = (
        P("layer", "row", "col"),
        P("layer", "col", "row"),
        P("layer", None),
        P("layer", None),
        P("layer"),
        P("row", "layer", "col"),
        P("row", "layer"),
    )
    return jax.shard_map(
        per_device, mesh=mesh, in_specs=in_specs, out_specs=P("row", "layer", "col"), check_vma=False
    )
```

time: 324 us -> 157 us (0.48)
  waiting for transfers between devices: 262 us -> 0 us
  Pallas kernels: 0 us -> 152 us
  matrix products: 20.3 us -> 0 us
  local copies, waits for them, and re-layouts: 21.2 us -> 3.54 us
  between operations: 13.8 us -> 0.66 us
  other arithmetic: 6.14 us -> 0 us
    all_gather x2 -> x0, waiting for transfers between devices: 194 us -> none  [the longest x1 101 us: per_device(): lower_full = lax.all_gather(lower_chosen, 'col', axis=2, tiled=True)]
    pallas_call x0 -> x1, Pallas kernels: none -> 152 us  [per_device(): pl.pallas_call(kernel, out_shape=jax.ShapeDtypeStruct((groups, cols), jnp...]
    reduce_scatter x1 -> x0, waiting for transfers between devices: 68.5 us -> none  [per_device(): lax.psum_scatter(lax.dot_general(reordered, upper_full, (((0, 2), (0, 2))...]
    dot_general x1 -> x0, matrix products: 20.3 us -> none  [per_device(): lax.dot_general(reordered, upper_full, (((0, 2), (0, 2)), ((), ())), pref...]
    reshape x1, local copies, waits for them, and re-layouts: 13.7 us -> 2.17 us  [per_device(): return updated.reshape(groups, 1, cols)]
    gather x2 -> x0, local copies, waits for them, and re-layouts: 5.66 us -> none  [the longest x1 2.83 us: per_device(): lower_chosen = jnp.take(lower_panels, lower_lists[0], axis=0)]
    select_n x4 -> x0, other arithmetic: 4.36 us -> none  [the longest x1 1.88 us: per_device(): jnp.where(live[:, None, None], lower_chosen, jnp.zeros((), lower_chosen.d...]
  transfers between devices with their start and end apart: 3 -> 0, of which waited for: 3 -> 0; matrix products, arithmetic and copies ran while one was open for 6% -> 0% of each run, Pallas kernels for 0% -> 0%
where the time goes in v1:
time: 157 us
  Pallas kernels  152 us (97%)
  local copies, waits for them, and re-layouts  3.54 us (2%)
    pallas_call x1, Pallas kernels, per_device(): pl.pallas_call(kernel, out_shape=jax.ShapeDtypeStruct((groups, cols), jnp...  152 us

profile of v1, /device:TPU:8, one launch (start us, length us, event | category | flops | bytes accessed | tf_op | source)
XLA Modules:
  0.0 156.6 jit_solution(13367494383205957653)
XLA Ops:
  0.7 1.4 copy.8.pivots
  2.0 152.4 %shard_map.73 = f32[80,1280]{1,0:T(8,128)} custom-call(s32[1,2]{1,0:T(1,128)} %lower_list.1, s32[1,2]{1,0:T(1,128)} %upper_list.1, s32[1]{0:T(128)S(6)} %copy.10.count, bf16[3,1280,512]{2,1,0:T(8,128)(2,1)} %lower_hbm.1, bf16[3,1280,512]{2,1,0:T(8,128)(2,1)} %upper_hbm.1, bf16[80,1280]{1,0:T(8,128)(2,1)} %bitcast.3, f32[80,1]{1,0:T(8,128)} %copy.8.pivots), custom_call_target="tpu_custom_call" | custom-call | flops 13421772800 | bytes 9437184 | tf_op jit(solution)/shard_map/pallas_call | solution.py:280
  154.4 2.2 %copy.9 = f32[80,1,1280]{2,1,0:T(1,128)} copy(f32[80,1,1280]{2,0,1:T(8,128)} %bitcast.2) | data formatting | bytes 819200 | tf_op jit(solution)/shard_map/reshape | solution.py:315

commit v2 on v1

v2 whole, which is shorter than its diff:
```python
import jax
import jax.numpy as jnp
from jax import lax
from jax.experimental import pallas as pl
from jax.experimental.pallas import tpu as pltpu
from jax.sharding import PartitionSpec as P

MESH = pl.DeviceIdType.MESH
GROUP = 128
CHUNKS = (256,) * 5
STRIPS = (1,) * 5
SPLIT = (0, 0, 0, 0, 1)
AHEAD = 1
STEPS = 5
NT = (((1,), (1,)), ((), ()))


def kernel(
    lower_list, upper_list, count, lower_hbm, upper_hbm, out,
    first_lower, first_upper, rest_lower, rest_upper, lower_all, upper_all, product, from_core, from_z,
    load_sem, own_send, own_recv, fwd_send, fwd_recv, core_send, core_recv, z_send, z_recv,
):
    layer, x, y = lax.axis_index("layer"), lax.axis_index("row"), lax.axis_index("col")
    z, core = lax.div(layer, 2), lax.rem(layer, 2)
    sign = 1 - 2 * core
    starts = [sum(CHUNKS[:i]) for i in range(len(CHUNKS))]
    last = len(CHUNKS) - 1
    ends = [sum(STRIPS[: s + 1]) for s in range(len(STRIPS))]
    edges = [0] + [sum(CHUNKS[:e]) for e in ends]
    first = CHUNKS[0]
    total_rows = lower_hbm.shape[1]

    loads = []
    for i, (hbm, head, rest) in enumerate(
        ((lower_hbm, first_lower, rest_lower), (upper_hbm, first_upper, rest_upper))
    ):
        loads.append(pltpu.make_async_copy(hbm.at[:, pl.ds(0, first)], head, load_sem.at[i, 0]))
        loads.append(
            pltpu.make_async_copy(hbm.at[:, pl.ds(first, total_rows - first)], rest, load_sem.at[i, 1])
        )
    for i in (0, 2, 1, 3):
        loads[i].start()

    def at_z(distance):
        return {"layer": lax.rem(layer + 2 * distance + 32, 16)}

    def at_ring(axis, step):
        return {"col": lax.rem(y + step + 4, 4)} if axis == 0 else {"row": lax.rem(x + step + 4, 4)}

    barrier = pltpu.get_barrier_semaphore()
    met = [at_ring(a, s) for a in (0, 1) for s in (1, -1)] + [{"layer": layer + sign}]
    met += [at_z(d) for d in (1, -1)]
    for target in met:
        pl.semaphore_signal(barrier, inc=1, device_id=target, device_id_type=MESH)

    position = lax.broadcasted_iota(jnp.int32, (GROUP, GROUP), 0)
    source = lax.broadcasted_iota(jnp.int32, (GROUP, GROUP), 1)
    wanted = (position % 8) * 16 + ((position // 8) % 8) * 2 + position // 64
    place = jnp.where(wanted == source, 1.0, 0.0).astype(jnp.bfloat16)
    buffers = (lower_all, upper_all)
    mine = (y, x)

    def prepare(i):
        low, up = (first_lower, first_upper) if i == 0 else (rest_lower, rest_upper)
        offset = 0 if i == 0 else first
        for slot in range(2):
            live = slot < count[0]
            lo, uo = lower_list[0, slot], upper_list[0, slot]
            for g in range(CHUNKS[i] // GROUP):
                row = starts[i] + g * GROUP
                rows = pl.ds(row - offset, GROUP)
                moved = jnp.dot(place, low[lo, rows, :], preferred_element_type=jnp.float32)
                moved = jnp.where(live, moved, 0.0)
                lower_all[y, slot, pl.ds(row, GROUP), :] = moved.astype(jnp.bfloat16)
                upper_all[x, slot, pl.ds(row, GROUP), :] = up[uo, rows, :]

    def own(axis, way, i, origin):
        step = 1 - 2 * way
        part = buffers[axis].at[origin, :, pl.ds(starts[i], CHUNKS[i]), :]
        return pltpu.make_async_remote_copy(
            part, part, own_send.at[axis, way, i], own_recv.at[axis, way, i],
            device_id=at_ring(axis, step), device_id_type=MESH,
        )

    def fwd(axis, way, i, origin):
        step = 1 - 2 * way
        part = buffers[axis].at[origin, way, pl.ds(starts[i], CHUNKS[i]), :]
        return pltpu.make_async_remote_copy(
            part, part, fwd_send.at[axis, way, i], fwd_recv.at[axis, way, i],
            device_id=at_ring(axis, step), device_id_type=MESH,
        )

    links = [(axis, way) for way in (0, 1) for axis in (0, 1)]

    def send_own(i):
        for axis, way in links:
            own(axis, way, i, mine[axis]).start()

    def pass_on(i):
        for axis, way in links:
            origin = lax.rem(mine[axis] - (1 - 2 * way) + 4, 4)
            own(axis, way, i, origin).wait_recv()
            fwd(axis, way, i, origin).start()

    def wait_far(i):
        for axis, way in links:
            fwd(axis, way, i, lax.rem(mine[axis] + 2, 4)).wait_recv()

    far = lax.rem(y + 2, 4)
    apart = lax.rem(x - y + 4, 4)
    half = lax.div(apart, 2)
    near_js = (lax.rem(far + 2 - half, 4), lax.rem(far + 3 - lax.div(apart, 3), 4))
    far_js = (far, lax.rem(far + jnp.maximum(apart, 1), 4))
    all_js = (0, 1, 2, 3)

    def block(row, rows, col, cols, js, more, keep):
        total = None
        for j in js:
            for slot in range(2):
                term = lax.dot_general(
                    lower_all[j, slot, pl.ds(row, rows), :], upper_all[j, slot, pl.ds(col, cols), :],
                    NT, preferred_element_type=jnp.float32,
                )
                total = term if total is None else total + term
        into, row0, col0 = keep
        for g in range(rows // GROUP):
            at = (slice(None), slice(None), pl.ds((row - row0) // 16 + g * 8, 8), pl.ds(col - col0, cols))
            piece = total[g * GROUP : (g + 1) * GROUP].reshape(2, 8, 8, cols)
            into[at] = into[at] + piece if more else piece

    def cut(end):
        return [(r, min(256, end - r)) for r in range(0, end, 256)]

    def multiply(i, js, more, done):
        begin, end = edges[i], edges[i + 1]
        for row, rows in cut(end):
            block(row, rows, begin, end - begin, js, more, (product[i][0], 0, begin))
        if done:
            to_core(i, 0).start()
            pending.append([i, 0, 0])
        for col, cols in cut(begin):
            block(begin, end - begin, col, cols, js, more, (product[i][1], begin, 0))
        if done and i:
            to_core(i, 1).start()
            pending.append([i, 1, 0])

    def rect(i, k):
        begin, end = edges[i], edges[i + 1]
        if k == 0:
            return pl.ds(0, end // 16), pl.ds(begin, end - begin)
        return pl.ds(begin // 16, (end - begin) // 16), pl.ds(0, begin)

    def to_core(i, k):
        return pltpu.make_async_remote_copy(
            product[i][k].at[1 - core], from_core[i][k],
            core_send.at[i, k], core_recv.at[i, k],
            device_id={"layer": layer + sign}, device_id_type=MESH,
        )

    def to_z(i, k, slot, target, hop):
        return pltpu.make_async_remote_copy(
            product[i][k].at[core, lax.rem(z + target + 16, 8)], from_z[i][k].at[slot],
            z_send.at[i, k, slot], z_recv.at[i, k, slot],
            device_id=at_z(hop), device_id_type=MESH,
        )

    def parts(i):
        return (0, 1) if i else (0,)

    def add_core(i, k):
        to_core(i, k).wait_recv()

        @pl.loop(0, 8)
        def _(t):
            product[i][k][core, t] = product[i][k][core, t] + from_core[i][k][t]

    def add_z(i, k, slot, target):
        at = lax.rem(z + target + 16, 8)
        product[i][k][core, at] = product[i][k][core, at] + from_z[i][k][slot]

    def advance(i, k, step):
        if step == 0:
            add_core(i, k)
        if step:
            to_z(i, k, step - 1, 0, sign).wait_recv()
            add_z(i, k, step - 1, sign * (4 - step))
        if step < 4:
            to_z(i, k, step, sign * (4 - step), sign).start()
        if 0 < step < 4:
            to_z(i, k, 3 + step, 0, -sign).wait_recv()
            add_z(i, k, 3 + step, -sign * (3 - step))
        if step < 3:
            to_z(i, k, 4 + step, -sign * (3 - step), -sign).start()

    pending = []

    def tick():
        for entry in list(pending):
            advance(*entry)
            entry[2] += 1
            if entry[2] == STEPS:
                pending.remove(entry)

    loads[0].wait()
    loads[2].wait()
    prepare(0)
    pl.semaphore_wait(barrier, len(met))
    send_own(0)
    loads[1].wait()
    loads[3].wait()
    for i in range(1, AHEAD):
        prepare(i)
        send_own(i)
    for i in range(last + 1):
        if i + AHEAD <= last:
            prepare(i + AHEAD)
            send_own(i + AHEAD)
        pass_on(i)
        tick()
        near = [s for s, end in enumerate(ends) if end == i + 1 and SPLIT[s]]
        for strip in near:
            multiply(strip, near_js, False, False)
        if i:
            wait_far(i - 1)
            tick()
        for strip, end in enumerate(ends):
            if end == i:
                multiply(strip, far_js if SPLIT[strip] else all_js, SPLIT[strip], True)
    wait_far(last)
    tick()
    multiply(len(STRIPS) - 1, far_js if SPLIT[-1] else all_js, SPLIT[-1], True)
    while pending:
        tick()

    for i in range(len(STRIPS)):
        for k in parts(i):
            rows, cols = rect(i, k)
            out[rows, cols] = product[i][k][core, z]

    for i in range(last + 1):
        for axis, way in links:
            own(axis, way, i, mine[axis]).wait_send()
            fwd(axis, way, i, lax.rem(mine[axis] - (1 - 2 * way) + 4, 4)).wait_send()
    for i in range(len(STRIPS)):
        for k in parts(i):
            to_core(i, k).wait_send()
            for slot in range(7):
                if slot < 4:
                    to_z(i, k, slot, sign * (4 - slot), sign).wait_send()
                else:
                    to_z(i, k, slot, -sign * (7 - slot), -sign).wait_send()


def per_device(
    lower_panels, upper_panels, lower_lists, upper_lists, block_counts, ancestor, pivot_inverse
):
    pool, rows, width = lower_panels.shape
    groups, _, cols = ancestor.shape
    chunks, strips = len(CHUNKS), len(STRIPS)
    smem = pl.BlockSpec(memory_space=pltpu.SMEM)
    vmem = pl.BlockSpec(memory_space=pltpu.VMEM)
    hbm = pl.BlockSpec(memory_space=pl.ANY)
    dma = pltpu.SemaphoreType.DMA

    def pieces(lead):
        shapes, begin = [], 0
        for i, count in enumerate(STRIPS):
            end = begin + sum(CHUNKS[sum(STRIPS[:i]) : sum(STRIPS[: i + 1])])
            down = pltpu.VMEM((*lead, end // 16, end - begin), jnp.float32)
            across = pltpu.VMEM((*lead, (end - begin) // 16, max(begin, 128)), jnp.float32)
            shapes.append((down, across) if begin else (down,))
            begin = end
        return tuple(shapes)

    total = pl.pallas_call(
        kernel,
        out_shape=jax.ShapeDtypeStruct((groups, cols), jnp.float32),
        in_specs=[smem, smem, smem, hbm, hbm],
        out_specs=vmem,
        scratch_shapes=[
            pltpu.VMEM((pool, CHUNKS[0], width), jnp.bfloat16),
            pltpu.VMEM((pool, CHUNKS[0], width), jnp.bfloat16),
            pltpu.VMEM((pool, rows - CHUNKS[0], width), jnp.bfloat16),
            pltpu.VMEM((pool, rows - CHUNKS[0], width), jnp.bfloat16),
            pltpu.VMEM((4, 2, rows, width), jnp.bfloat16),
            pltpu.VMEM((4, 2, cols, width), jnp.bfloat16),
            pieces((2, 8)),
            pieces((8,)),
            pieces((7,)),
            dma((2, 2)),
            dma((2, 2, chunks)),
            dma((2, 2, chunks)),
            dma((2, 2, chunks)),
            dma((2, 2, chunks)),
            dma((strips, 2)),
            dma((strips, 2)),
            dma((strips, 2, 7)),
            dma((strips, 2, 7)),
        ],
        compiler_params=pltpu.CompilerParams(
            collective_id=0, has_side_effects=True, vmem_limit_bytes=58 * 2**20
        ),
        cost_estimate=pl.CostEstimate(
            flops=4 * rows * cols * width * 4, bytes_accessed=9 * 2**20, transcendentals=0
        ),
    )(
        lower_lists, upper_lists, block_counts, lower_panels, upper_panels,
    )
    return (ancestor.astype(jnp.float32) - total.reshape(groups, 1, cols)) * pivot_inverse[:, :, None]


def solution(mesh):
    in_specs = (
        P("layer", "row", "col"),
        P("layer", "col", "row"),
        P("layer", None),
        P("layer", None),
        P("layer"),
        P("row", "layer", "col"),
        P("row", "layer"),
    )
    return jax.shard_map(
        per_device, mesh=mesh, in_specs=in_specs, out_specs=P("row", "layer", "col"), check_vma=False
    )
```

time: 157 us -> 128 us (0.82)
  Pallas kernels: 152 us -> 124 us
  local copies, waits for them, and re-layouts: 3.54 us -> 1.18 us
    pallas_call x1, Pallas kernels: 152 us -> 124 us  [per_device(): pl.pallas_call(kernel, out_shape=jax.ShapeDtypeStruct((groups, cols), jnp...]
    reshape x1 -> x0, local copies, waits for them, and re-layouts: 2.17 us -> none  [per_device(): return updated.reshape(groups, 1, cols)]
where the time goes in v2:
time: 128 us; the launch traced here: 127 us
  Pallas kernels  124 us (97%)
    pallas_call x1, Pallas kernels, per_device(): pl.pallas_call(kernel, out_shape=jax.ShapeDtypeStruct((groups, cols), jnp...  124 us

profile of v2, /device:TPU:8, one launch (start us, length us, event | category | flops | bytes accessed | tf_op | source)
XLA Modules:
  0.0 127.2 jit_solution(10648917211020739034)
XLA Ops:
  0.7 0.0 copy-start
  0.7 0.0 copy-start.1
  0.7 124.3 %shard_map.73 = f32[80,1280]{1,0:T(8,128)} custom-call(s32[1,2]{1,0:T(1,128)} %lower_list.1, s32[1,2]{1,0:T(1,128)} %upper_list.1, s32[1]{0:T(128)S(6)} %copy.9.count, bf16[3,1280,512]{2,1,0:T(8,128)(2,1)} %lower_hbm.1, bf16[3,1280,512]{2,1,0:T(8,128)(2,1)} %upper_hbm.1), custom_call_target="tpu_custom_call" | custom-call | flops 13421772800 | bytes 9437184 | tf_op jit(solution)/shard_map/pallas_call | solution.py:275
  124.9 0.0 copy-done
  125.0 0.0 copy-done.1
  125.0 1.1 fusion
  126.1 1.2 copy.8
Async XLA Ops:
  0.7 124.3 %copy-start = (bf16[80,1,1280]{2,0,1:T(8,128)(2,1)S(1)}, bf16[80,1,1280]{2,0,1:T(8,128)(2,1)}, u32[]{:S(2)}) copy-start(bf16[80,1,1280]{2,0,1:T(8,128)(2,1)} %param.12) | copy-start | bytes 614404
  0.7 124.3 %copy-start.1 = (f32[80,1]{0,1:T(1,128)S(1)}, f32[80,1]{0,1:T(1,128)}, u32[]{:S(2)}) copy-start(f32[80,1]{0,1:T(1,128)} %param.13) | copy-start | bytes 964

commit v3 on v2

--- a/solution.py
+++ b/solution.py
@@ -220,6 +220,7 @@
         near = [s for s, end in enumerate(ends) if end == i + 1 and SPLIT[s]]
         for strip in near:
             multiply(strip, near_js, False, False)
+            tick()
         if i:
             wait_far(i - 1)
             tick()

time: 128 us -> 131 us (1.023)
  Pallas kernels: 124 us -> 127 us
    pallas_call x1, Pallas kernels: 124 us -> 127 us  [per_device(): pl.pallas_call(kernel, out_shape=jax.ShapeDtypeStruct((groups, cols), jnp...]
where the time goes in v3:
time: 131 us; the launch traced here: 130 us
  Pallas kernels  127 us (97%)
    pallas_call x1, Pallas kernels, per_device(): pl.pallas_call(kernel, out_shape=jax.ShapeDtypeStruct((groups, cols), jnp...  127 us

profile of v3, /device:TPU:8, one launch (start us, length us, event | category | flops | bytes accessed | tf_op | source)
XLA Modules:
  0.0 130.1 jit_solution(15562723618885448315)
XLA Ops:
  0.7 0.0 copy-start
  0.7 0.0 copy-start.1
  0.7 127.1 %shard_map.73 = f32[80,1280]{1,0:T(8,128)} custom-call(s32[1,2]{1,0:T(1,128)} %lower_list.1, s32[1,2]{1,0:T(1,128)} %upper_list.1, s32[1]{0:T(128)S(6)} %copy.9.count, bf16[3,1280,512]{2,1,0:T(8,128)(2,1)} %lower_hbm.1, bf16[3,1280,512]{2,1,0:T(8,128)(2,1)} %upper_hbm.1), custom_call_target="tpu_custom_call" | custom-call | flops 13421772800 | bytes 9437184 | tf_op jit(solution)/shard_map/pallas_call | solution.py:276
  127.8 0.0 copy-done
  127.8 0.0 copy-done.1
  127.8 1.1 fusion
  128.9 1.2 copy.8
Async XLA Ops:
  0.7 127.1 %copy-start = (bf16[80,1,1280]{2,0,1:T(8,128)(2,1)S(1)}, bf16[80,1,1280]{2,0,1:T(8,128)(2,1)}, u32[]{:S(2)}) copy-start(bf16[80,1,1280]{2,0,1:T(8,128)(2,1)} %param.12) | copy-start | bytes 614404
  0.7 127.1 %copy-start.1 = (f32[80,1]{0,1:T(1,128)S(1)}, f32[80,1]{0,1:T(1,128)}, u32[]{:S(2)}) copy-start(f32[80,1]{0,1:T(1,128)} %param.13) | copy-start | bytes 964
